TPU v7x, 32 devices: a whole 2x2x4 slice. The times are simulated.
32 devices in a mesh: grp: 4 (over y, x), mdl: 8 (over z, core).
Axes of the slice: x: 2, y: 2, z: 4, core: 2. Of those that a mesh axis runs over, the one named last changes fastest.
Arguments:
- pol_hidden: bfloat16 [128, 4096], P(('grp', 'mdl')), may hold values from -6 to 6
- ref_hidden: bfloat16 [128, 4096], P(('grp', 'mdl')), may hold values from -6 to 6
- pol_mlp_gain: bfloat16 [4096], replicated, may hold values from 0.099609375 to 1.8984375
- ref_mlp_gain: bfloat16 [4096], replicated, may hold values from 0.099609375 to 1.8984375
- pol_final_gain: bfloat16 [4096], replicated, may hold values from 0.099609375 to 1.8984375
- ref_final_gain: bfloat16 [4096], replicated, may hold values from 0.099609375 to 1.8984375
- pol_gate: bfloat16 [4096, 11008], P(None, 'mdl'), may hold values from -0.09375 to 0.09375
- pol_up: bfloat16 [4096, 11008], P(None, 'mdl'), may hold values from -0.09375 to 0.09375
- pol_down: bfloat16 [11008, 4096], P('mdl'), may hold values from -0.109375 to 0.109375
- ref_gate: bfloat16 [4096, 11008], P(None, 'mdl'), may hold values from -0.09375 to 0.09375
- ref_up: bfloat16 [4096, 11008], P(None, 'mdl'), may hold values from -0.09375 to 0.09375
- ref_down: bfloat16 [11008, 4096], P('mdl'), may hold values from -0.109375 to 0.109375
- pol_head: bfloat16 [64000, 4096], P(('grp', 'mdl')), may hold values from -20 to 20
- ref_head: bfloat16 [64000, 4096], P(('grp', 'mdl')), may hold values from -20 to 20
- token_ids: int32 [128], replicated, may hold values from 0 to 63999
- lengths: int32 [16], replicated, may hold values from 1 to 32, 128 in all
Outputs:
- pol_out: bfloat16 [128, 4096], P(('grp', 'mdl'))
- ref_out: bfloat16 [128, 4096], P(('grp', 'mdl'))
- rollout_ratio: float32 [16], replicated
Inputs may be any that keep to these rules, and one draw needn't show every extreme that they name: Rollout lengths sum to 128; the longest is exactly 32.
All inputs are finite; a program needn't handle non-finite values.
Results may differ from a plain program's by a relative error of at most 0.012.
The roundings to bfloat16 on the way count: a program that leaves them out, or rounds other values in their place, can miss the bound.
Values may be sent and summed in bfloat16 or wider, within the bound.
A program may use at most 192 MiB of HBM per device.

v0:
```python
import jax
import jax.numpy as jnp
from jax import lax
from jax.sharding import PartitionSpec as P


def rms_rows(rows, gain):
    values = rows.astype(jnp.float32)
    scale = lax.rsqrt(jnp.mean(values * values, axis=-1, keepdims=True) + 1e-05)
    return (values * scale * gain.astype(jnp.float32)).astype(jnp.bfloat16)


def mlp_hidden(piece, gain, w_gate, w_up):
    normed = rms_rows(piece, gain)
    gate = jnp.dot(normed, w_gate, preferred_element_type=jnp.float32)
    upper = jnp.dot(normed, w_up, preferred_element_type=jnp.float32)
    return (jax.nn.silu(gate) * upper).astype(jnp.bfloat16)


def vocab_terms(token_rows, head_rows, targets, vocab):
    logits = jnp.einsum("td,vd->tv", token_rows, head_rows, preferred_element_type=jnp.float32)
    peak = jnp.max(logits, axis=1)
    total = jnp.sum(jnp.exp(logits - peak[:, None]), axis=1)
    target = jnp.sum(jnp.where(targets[:, None] == vocab[None, :], logits, 0.0), axis=1)
    return (peak, total, target)


def rollout_totals(log_ratio, positions, lengths):
    ends = jnp.cumsum(lengths)
    owner = jnp.sum((positions[:, None] >= ends[None, :]).astype(jnp.int32), axis=1)
    onehot = (owner[:, None] == jnp.arange(lengths.shape[0], dtype=jnp.int32)[None, :]).astype(
        jnp.float32
    )
    return jnp.sum(log_ratio[:, None] * onehot, axis=0)


def per_device(
    pol_hidden,
    ref_hidden,
    pol_mlp_gain,
    ref_mlp_gain,
    pol_final_gain,
    ref_final_gain,
    pol_gate,
    pol_up,
    pol_down,
    ref_gate,
    ref_up,
    ref_down,
    pol_head,
    ref_head,
    token_ids,
    lengths,
):
    results = []
    models = (
        (pol_hidden, pol_mlp_gain, pol_gate, pol_up, pol_down),
        (ref_hidden, ref_mlp_gain, ref_gate, ref_up, ref_down),
    )
    for hidden_in, gain, w_gate, w_up, w_down in models:

        def expand(piece, start, gain=gain, w_gate=w_gate, w_up=w_up):
            return mlp_hidden(piece, gain, w_gate, w_up)

        hidden = expand(lax.all_gather(hidden_in, "mdl", axis=0, tiled=True), jnp.int32(0))

        def project(start, count, hidden=hidden, w_down=w_down):
            return jnp.dot(hidden, w_down, preferred_element_type=jnp.float32)

        mixed = lax.psum_scatter(
            project(jnp.int32(0), hidden_in.shape[0] * lax.axis_size("mdl")),
            "mdl",
            scatter_dimension=0,
            tiled=True,
        )
        results.append((hidden_in.astype(jnp.float32) + mixed).astype(jnp.bfloat16))
    finals = [rms_rows(results[0], pol_final_gain), rms_rows(results[1], ref_final_gain)]
    voc_dev = pol_head.shape[0]
    members = lax.axis_size("mdl")
    group = lax.axis_index("grp")
    member = lax.axis_index("mdl")
    pol_rows, ref_rows = (
        lax.all_gather(finals[0], ("grp", "mdl"), axis=0, tiled=True),
        lax.all_gather(finals[1], ("grp", "mdl"), axis=0, tiled=True),
    )
    positions = jnp.arange(pol_rows.shape[0], dtype=jnp.int32)
    vocab = (group * members + member) * voc_dev + jnp.arange(voc_dev, dtype=jnp.int32)
    pol_terms = vocab_terms(pol_rows, pol_head, token_ids, vocab)
    ref_terms = vocab_terms(ref_rows, ref_head, token_ids, vocab)
    peaks = lax.pmax((pol_terms[0], ref_terms[0]), ("grp", "mdl"))
    sums = lax.psum(
        (
            pol_terms[1] * jnp.exp(pol_terms[0] - peaks[0]),
            pol_terms[2],
            ref_terms[1] * jnp.exp(ref_terms[0] - peaks[1]),
            ref_terms[2],
        ),
        ("grp", "mdl"),
    )
    pol_logp = sums[1] - peaks[0] - jnp.log(sums[0])
    ref_logp = sums[3] - peaks[1] - jnp.log(sums[2])
    rollout_ratio = rollout_totals(pol_logp - ref_logp, positions, lengths)
    return (results[0], results[1], rollout_ratio)


def solution(mesh):
    placed = (
        P(("grp", "mdl"), None),
        P(("grp", "mdl"), None),
        P(),
        P(),
        P(),
        P(),
        P(None, "mdl"),
        P(None, "mdl"),
        P("mdl", None),
        P(None, "mdl"),
        P(None, "mdl"),
        P("mdl", None),
        P(("grp", "mdl"), None),
        P(("grp", "mdl"), None),
        P(),
        P(),
    )
    return jax.shard_map(
        per_device,
        mesh=mesh,
        in_specs=placed,
        out_specs=(P(("grp", "mdl"), None), P(("grp", "mdl"), None), P()),
        check_vma=False,
    )
```

profile of v0, /device:TPU:0, one launch (start us, length us, event | category | flops | bytes accessed | tf_op | source)
XLA Modules:
  0.0 351.3 jit_solution(15834408972016230710)
XLA Ops:
  7.2 0.0 all-reduce.7.cloned.1.call-start
  7.2 16.1 %all-gather.1 = bf16[8,4,4096]{2,1,0:T(4,128)(2,1)S(1)} all-gather(bf16[1,4,4096]{2,1,0:T(4,128)(2,1)} %bitcast.19), channel_id=1, replica_groups=mesh['grp'=4,'mdl'=8] {'mdl'}, dimensions={0}, use_global_device_ids=true | all-gather | bytes 294912 | tf_op jit(solution)/shard_map/all_gather | solution.py:65
  23.4 0.2 multiply_reduce_fusion
  23.5 0.7 convert_element_type.66
  24.2 14.4 %all-gather = bf16[8,4,4096]{2,1,0:T(4,128)(2,1)S(1)} all-gather(bf16[1,4,4096]{2,1,0:T(4,128)(2,1)} %bitcast.18), channel_id=1, replica_groups=mesh['grp'=4,'mdl'=8] {'mdl'}, dimensions={0}, use_global_device_ids=true | all-gather | bytes 294912 | tf_op jit(solution)/shard_map/all_gather | solution.py:65
  38.6 0.2 multiply_reduce_fusion.1
  38.8 0.7 convert_element_type.60
  39.5 7.5 %fusion.31 = f32[32,1376]{1,0:T(8,128)S(1)} fusion(bf16[4096,1376]{0,1:T(8,128)(2,1)} %param.25, f32[32,4096]{1,0:T(8,128)S(1)} %reshape.86, f32[4096]{0:T(1024)S(1)} %convert_element_type.66, f32[32]{0:T(128)S(1)} %add_rsqrt_fusion.2), kind=kOutput, calls=%fused_computation.59 | convolution fusion | flops 361103360 | bytes 11989120 | tf_op jit(solution)/shard_map/dot_general | solution.py:15
  47.1 13.9 %fusion.4 = f32[32,4096]{1,0:T(8,128)} fusion(bf16[1376,4096]{1,0:T(8,128)(2,1)} %param.27, bf16[4096,1376]{0,1:T(8,128)(2,1)} %param.26, f32[32,1376]{1,0:T(8,128)S(1)} %fusion.31, f32[32,4096]{1,0:T(8,128)S(1)} %reshape.86, f32[4096]{0:T(1024)S(1)} %convert_element_type.66, f32[32]{0:T(128)S(1)} %add_rsqrt_fusion.2), kind=kOutput, calls=%fused_computation.10 | convolution fusion | flops 722077696 | bytes 23785600 | tf_op jit(solution)/shard_map/dot_general | solution.py:68
  61.0 7.5 %fusion.30 = f32[32,1376]{1,0:T(8,128)S(1)} fusion(bf16[4096,1376]{0,1:T(8,128)(2,1)} %param.22, f32[32,4096]{1,0:T(8,128)S(1)} %reshape.85, f32[4096]{0:T(1024)S(1)} %convert_element_type.60, f32[32]{0:T(128)S(1)} %add_rsqrt_fusion.3), kind=kOutput, calls=%fused_computation.58 | convolution fusion | flops 361103360 | bytes 11989120 | tf_op jit(solution)/shard_map/dot_general | solution.py:15
  68.5 0.0 copy-start.4
  68.5 0.0 copy-start.8
  68.5 0.0 copy-start
  68.5 0.0 copy-start.1
  68.6 0.0 copy-start.5
  68.6 0.0 copy-start.7
  68.6 14.1 %fusion.5 = f32[32,4096]{1,0:T(8,128)} fusion(bf16[1376,4096]{1,0:T(8,128)(2,1)} %param.24, bf16[4096,1376]{0,1:T(8,128)(2,1)} %param.23, f32[32,1376]{1,0:T(8,128)S(1)} %fusion.30, f32[32,4096]{1,0:T(8,128)S(1)} %reshape.85, f32[4096]{0:T(1024)S(1)} %convert_element_type.60, f32[32]{0:T(128)S(1)} %add_rsqrt_fusion.3), kind=kOutput, calls=%fused_computation.11 | convolution fusion | flops 722077696 | bytes 23785600 | tf_op jit(solution)/shard_map/dot_general | solution.py:68
  82.7 0.0 all-reduce.7.cloned.1.call-update
  82.7 0.0 all-gather.9.cloned.1.call-start
  82.7 0.0 copy-done.4
  82.8 0.0 copy-done.8
  82.8 0.6 dynamic-slice
  84.0 58.9 %all-reduce.7.cloned.1.call-done = (f32[32,4096]{1,0:T(8,128)}, f32[32,4096]{1,0:T(8,128)}) async-done(((f32[32,4096]{1,0:T(8,128)}, f32[32,4096]{1,0:T(8,128)}), (f32[32,4096]{1,0:T(8,128)}, f32[32,4096]{1,0:T(8,128)})) %all-reduce.7.cloned.1.call-update) | async-done | bytes 1048592
  143.0 0.0 copy-done
  143.0 0.0 copy-done.1
  143.0 1.2 fusion.18
  144.2 0.0 copy-start.2
  144.2 0.0 copy-start.3
  144.2 0.7 fusion.26
  144.9 0.0 all-gather.9.cloned.1.call-update
  144.9 0.0 all-gather.7.cloned.1.call-start
  145.0 0.0 copy-done.5
  145.0 0.7 fusion.27
  145.7 0.0 all-gather.7.cloned.1.call-update
  145.7 0.0 copy-done.7
  145.7 0.1 copy.22
  145.8 0.1 reduce
  146.0 0.1 convert_reduce_fusion
  146.1 52.7 %all-gather.9.cloned.1.call-done = bf16[32,4,4096]{2,1,0:T(4,128)(2,1)} async-done(((bf16[1,4,4096]{2,1,0:T(4,128)(2,1)}), bf16[32,4,4096]{2,1,0:T(4,128)(2,1)}) %all-gather.9.cloned.1.call-update) | async-done | bytes 1048592 | tf_op jit(solution)/shard_map/all_gather | solution.py:84
  198.8 1.3 reshape.84
  200.1 8.0 %fusion.35 = (f32[128]{0:T(128)S(1)}, f32[128,2000]{0,1:T(8,128)S(1)}) fusion(bf16[128,4096]{1,0:T(8,128)(2,1)S(1)} %reshape.84, bf16[2000,4096]{1,0:T(8,128)(2,1)} %param.29), kind=kOutput, calls=%fused_computation.61 | convolution fusion | flops 2097407872 | bytes 18457088 | tf_op jit(solution)/shard_map/td,vd->tv/dot_general | solution.py:21
  208.1 0.0 copy-done.2
  208.1 0.0 copy-done.3
  208.1 46.5 %all-gather.7.cloned.1.call-done = bf16[32,4,4096]{2,1,0:T(4,128)(2,1)} async-done(((bf16[1,4,4096]{2,1,0:T(4,128)(2,1)}), bf16[32,4,4096]{2,1,0:T(4,128)(2,1)}) %all-gather.7.cloned.1.call-update) | async-done | bytes 1048592 | tf_op jit(solution)/shard_map/all_gather | solution.py:83
  254.6 1.3 reshape.82
  255.9 0.0 copy-start.6
  255.9 8.0 %fusion.34 = (f32[128]{0:T(128)S(1)}, f32[128,2000]{0,1:T(8,128)S(1)}) fusion(bf16[128,4096]{1,0:T(8,128)(2,1)S(1)} %reshape.82, bf16[2000,4096]{1,0:T(8,128)(2,1)} %param.28), kind=kOutput, calls=%fused_computation.60 | convolution fusion | flops 2097407872 | bytes 18457088 | tf_op jit(solution)/shard_map/td,vd->tv/dot_general | solution.py:21
  263.9 39.5 %all-reduce.3 = (f32[128]{0:T(128)S(1)}, f32[128]{0:T(128)S(1)}) all-reduce(f32[128]{0:T(128)S(1)} %get-tuple-element.23, f32[128]{0:T(128)S(1)} %get-tuple-element.21), channel_id=1, replica_groups=mesh['grp'=4,'mdl'=8] {'grp','mdl'}, use_global_device_ids=true, to_apply=%region_17.18 | all-reduce | flops 256 | bytes 2048 | tf_op jit(solution)/shard_map/pmax | solution.py:90
  303.4 0.0 copy-done.6
  303.4 0.9 fusion.2
  304.4 39.8 %all-reduce.2 = (f32[128]{0:T(128)S(1)}, f32[128]{0:T(128)S(1)}, f32[128]{0:T(128)S(1)}, f32[128]{0:T(128)S(1)}) all-reduce(f32[128]{0:T(128)S(1)} %exponential_multiply_fusion, f32[128]{0:T(128)S(1)} %get-tuple-element.8, f32[128]{0:T(128)S(1)} %exponential_multiply_fusion.1, ...), channel_id=1, replica_groups=mesh['grp'=4,'mdl'=8] {'grp','mdl'}, use_global_device_ids=true, to_apply=%region_19.20 | all-reduce | flops 512 | bytes 4096 | tf_op jit(solution)/shard_map/psum | solution.py:91
  344.2 0.6 select_reduce_fusion
  (13 shorter events, 0.2 us)
Async XLA Ops:
  7.2 135.8 %all-reduce.7.cloned.1.call-start = ((), (), s32[]{:S(2)}) async-start(), calls=%async_computation.2 | async-start | bytes 2097152
  68.5 14.2 %copy-start.4 = (bf16[4096]{0:T(1024)(128)(2,1)S(1)}, bf16[4096]{0:T(1024)(128)(2,1)}, u32[]{:S(2)}) copy-start(bf16[4096]{0:T(1024)(128)(2,1)} %param.21) | copy-start | bytes 24580
  68.5 14.3 %copy-start.8 = (u32[32]{0:T(128)S(1)}, u32[32]{0:T(128)}, u32[]{:S(2)}) copy-start(u32[32]{0:T(128)} %constant.42) | copy-start | bytes 388
  68.5 74.4 %copy-start = (bf16[4,4096]{1,0:T(4,128)(2,1)S(1)}, bf16[4,4096]{1,0:T(4,128)(2,1)}, u32[]{:S(2)}) copy-start(bf16[4,4096]{1,0:T(4,128)(2,1)} %param.16) | copy-start | bytes 98308
  68.5 74.4 %copy-start.1 = (bf16[4,4096]{1,0:T(4,128)(2,1)S(1)}, bf16[4,4096]{1,0:T(4,128)(2,1)}, u32[]{:S(2)}) copy-start(bf16[4,4096]{1,0:T(4,128)(2,1)} %param.17) | copy-start | bytes 98308
  68.6 76.4 %copy-start.5 = (bf16[4096]{0:T(1024)(128)(2,1)S(1)}, bf16[4096]{0:T(1024)(128)(2,1)}, u32[]{:S(2)}) copy-start(bf16[4096]{0:T(1024)(128)(2,1)} %param.20) | copy-start | bytes 24580
  68.6 77.1 %copy-start.7 = (s32[16]{0:T(128)S(1)}, s32[16]{0:T(128)}, u32[]{:S(2)}) copy-start(s32[16]{0:T(128)} %param.31) | copy-start | bytes 196
  82.7 116.1 %all-gather.9.cloned.1.call-start = ((), (), s32[]{:S(2)}) async-start(), calls=%async_computation.1 | async-start | bytes 1081344 | tf_op jit(solution)/shard_map/all_gather | solution.py:84
  144.2 63.9 %copy-start.2 = (bf16[4,4096]{1,0:T(4,128)(2,1)}, bf16[4,4096]{1,0:T(4,128)(2,1)S(1)}, u32[]{:S(2)}) copy-start(bf16[4,4096]{1,0:T(4,128)(2,1)S(1)} %get-tuple-element.20) | copy-start | bytes 98308
  144.2 63.9 %copy-start.3 = (bf16[4,4096]{1,0:T(4,128)(2,1)}, bf16[4,4096]{1,0:T(4,128)(2,1)S(1)}, u32[]{:S(2)}) copy-start(bf16[4,4096]{1,0:T(4,128)(2,1)S(1)} %get-tuple-element.26) | copy-start | bytes 98308
  144.9 109.7 %all-gather.7.cloned.1.call-start = ((), (), s32[]{:S(2)}) async-start(), calls=%async_computation | async-start | bytes 1081344 | tf_op jit(solution)/shard_map/all_gather | solution.py:83
  255.9 47.5 %copy-start.6 = (s32[128]{0:T(128)S(1)}, s32[128]{0:T(128)}, u32[]{:S(2)}) copy-start(s32[128]{0:T(128)} %param.30) | copy-start | bytes 1540
Sparse Core Ops, SparseCore 0:
  82.8 60.1 all-reduce.6
  146.0 52.7 all-gather.8
  201.8 52.7 all-gather.6
where the time goes:
time: 352 us; the launch traced here: 351 us
  waiting for transfers between devices  158 us (45%)
  blocking collectives  110 us (31%)
  matrix products  59 us (17%)
  between operations  14.6 us (4%)
  other arithmetic  6.16 us (2%)
    unnamed x4, waiting for transfers between devices  59 us
    all_gather x1, waiting for transfers between devices, per_device(): lax.all_gather(finals[1], ('grp', 'mdl'), axis=0, tiled=True)  52.7 us
    all_gather x1, waiting for transfers between devices, per_device(): lax.all_gather(finals[0], ('grp', 'mdl'), axis=0, tiled=True)  46.5 us
    psum x1, blocking collectives, per_device(): lax.psum((pol_terms[1] * jnp.exp(pol_terms[0] - peaks[0]), pol_terms[2],...  39.8 us
    pmax x1, blocking collectives, per_device(): peaks = lax.pmax((pol_terms[0], ref_terms[0]), ('grp', 'mdl'))  39.5 us
    all_gather x2, blocking collectives, per_device(): lax.all_gather(hidden_in, 'mdl', axis=0, tiled=True)  30.5 us
    dot_general x2, matrix products, project(): return jnp.dot(hidden, w_down, preferred_element_type=jnp.float32)  28 us
    dot_general x2, matrix products, vocab_terms(): jnp.einsum('td,vd->tv', token_rows, head_rows, preferred_element_type=jnp...  16 us
  transfers between devices with their start and end apart: 3, of which 3 were waited for; matrix products, arithmetic and copies ran while one was open for 3% of the time, Pallas kernels for 0%

commit v1 on v0

--- a/solution.py
+++ b/solution.py
@@ -1,7 +1,16 @@
+import functools
+
 import jax
 import jax.numpy as jnp
 from jax import lax
+from jax.experimental import pallas as pl
+from jax.experimental.pallas import tpu as pltpu
 from jax.sharding import PartitionSpec as P
+
+MESH = pl.DeviceIdType.MESH
+DEPTH = 4
+EARLY = 2
+VMEM_LIMIT = 62 * 1024 * 1024
 
 
 def rms_rows(rows, gain):
@@ -26,7 +35,8 @@
 
 
 def rollout_totals(log_ratio, positions, lengths):
-    ends = jnp.cumsum(lengths)
+    order = jnp.arange(lengths.shape[0], dtype=jnp.int32)
+    ends = jnp.sum(jnp.where(order[None, :] <= order[:, None], lengths[None, :], 0), axis=1)
     owner = jnp.sum((positions[:, None] >= ends[None, :]).astype(jnp.int32), axis=1)
     onehot = (owner[:, None] == jnp.arange(lengths.shape[0], dtype=jnp.int32)[None, :]).astype(
         jnp.float32
@@ -103,6 +113,424 @@
     return (results[0], results[1], rollout_ratio)
 
 
+def fused_kernel(
+    n_grp, n_mdl, n_k, n_head,
+    pol_hid, ref_hid, pol_mg, ref_mg, pol_fg, ref_fg,
+    pol_gate, pol_up, pol_down, ref_gate, ref_up, ref_down,
+    pol_head, ref_head, ids, lengths,
+    pol_out, ref_out, ratio_out,
+    hid, xs, xraw, acc_g, acc_u, hbuf, ring_a, ring_b, heads,
+    rs_send, rs_recv, own_part, yall, fin, st_send, st1, st2,
+    sem_a, sem_b, sem_h, hs_sem, hr_sem, rss_sem, rsr_sem,
+    zs_sem, xs_sem, cs_sem, yr_sem, s1s_sem, s1r_sem, s2s_sem, s2r_sem,
+):
+    g = lax.axis_index("grp")
+    m = lax.axis_index("mdl")
+    n_z = n_mdl // 2
+    tg = xs.shape[2]
+    kc = xs.shape[3]
+    d = pol_gate.shape[0]
+    cb = d // n_mdl
+    quarter = d // 4
+    hc = pol_head.shape[0] // n_head
+    gates, ups, downs = (pol_gate, ref_gate), (pol_up, ref_up), (pol_down, ref_down)
+    head_refs = (pol_head, ref_head)
+    hids, mgs, fgs = (pol_hid, ref_hid), (pol_mg, ref_mg), (pol_fg, ref_fg)
+    outs = (pol_out, ref_out)
+
+    def copy_a(mod, k):
+        slot = lax.rem(k, DEPTH) * 2
+        rows = pl.ds(pl.multiple_of(k * kc, kc), kc)
+        return (
+            pltpu.make_async_copy(gates[mod].at[rows, :], ring_a.at[slot], sem_a.at[slot]),
+            pltpu.make_async_copy(ups[mod].at[rows, :], ring_a.at[slot + 1], sem_a.at[slot + 1]),
+        )
+
+    def start_a(mod, k):
+        for c in copy_a(mod, k):
+            c.start()
+
+    def copy_b(mod, j):
+        peer = lax.rem(m + 1 + j, n_mdl)
+        cols = pl.ds(pl.multiple_of(peer * cb, cb), cb)
+        return pltpu.make_async_copy(downs[mod].at[:, cols], ring_b.at[j], sem_b.at[j])
+
+    def copy_h(mod, c):
+        rows = pl.ds(pl.multiple_of(c * hc, hc), hc)
+        return pltpu.make_async_copy(head_refs[mod].at[rows, :], heads.at[mod, c], sem_h.at[mod, c])
+
+    def remote(src, dst, ssem, rsem, dg, dm):
+        return pltpu.make_async_remote_copy(
+            src_ref=src, dst_ref=dst, send_sem=ssem, recv_sem=rsem,
+            device_id=(dg, dm), device_id_type=MESH,
+        )
+
+    def loop(n, body, start=0):
+        def step(i, carry):
+            body(i)
+            return carry
+
+        lax.fori_loop(start, n, step, 0)
+
+    loop(DEPTH, lambda k: start_a(0, k))
+    loop(n_mdl, lambda j: copy_b(0, j).start())
+    loop(EARLY, lambda c: copy_h(0, c).start())
+
+    barrier = pltpu.get_barrier_semaphore()
+    for i in range(1, n_mdl):
+        pl.semaphore_signal(barrier, inc=1, device_id=(g, lax.rem(m + i, n_mdl)), device_id_type=MESH)
+    for i in range(1, n_grp):
+        pl.semaphore_signal(barrier, inc=1, device_id=(lax.rem(g + i, n_grp), m), device_id_type=MESH)
+    pl.semaphore_wait(barrier, n_mdl + n_grp - 2)
+
+    def hid_rows(mod, who):
+        return hid.at[mod, pl.ds(pl.multiple_of(who * 16, 16), 16)]
+
+    def hid_copy(mod, i, sender):
+        peer = lax.rem(m + 1 + i, n_mdl)
+        return remote(hids[mod], hid_rows(mod, sender), hs_sem.at[mod, i], hr_sem.at[mod, sender], g, peer)
+
+    for mod in (0, 1):
+        loop(n_mdl - 1, lambda i, mod=mod: hid_copy(mod, i, m).start())
+        hid[mod, pl.ds(pl.multiple_of(m * 16, 16), 16)] = hids[mod][...]
+
+    def normed_input(mod):
+        loop(n_mdl - 1, lambda i: hid_copy(mod, i, lax.rem(m + 1 + i, n_mdl)).wait_recv())
+        stacked = hid[mod]
+        t = lax.broadcasted_iota(jnp.int32, (tg, n_mdl * 16), 0)
+        r = lax.broadcasted_iota(jnp.int32, (tg, n_mdl * 16), 1)
+        parts = []
+        total = jnp.zeros((tg, 1), jnp.float32)
+        for q in range(4):
+            pick = (r == t * 4 + q).astype(jnp.bfloat16)
+            part = jnp.dot(pick, stacked, preferred_element_type=jnp.float32)
+            total += jnp.sum(part * part, axis=1, keepdims=True)
+            parts.append(part)
+        scale = lax.rsqrt(total / d + 1e-05)
+        for q in range(4):
+            gain = mgs[mod][:, q * quarter:(q + 1) * quarter].astype(jnp.float32)
+            normed = (parts[q] * scale * gain).astype(jnp.bfloat16)
+            raw = parts[q].astype(jnp.bfloat16)
+            for b in range(quarter // kc):
+                xs[mod, q * (quarter // kc) + b] = normed[:, b * kc:(b + 1) * kc]
+            for b in range(quarter // cb):
+                xraw[mod, q * (quarter // cb) + b] = raw[:, b * cb:(b + 1) * cb]
+
+    def expand_step(mod, k, first):
+        for c in copy_a(mod, k):
+            c.wait()
+        slot = lax.rem(k, DEPTH) * 2
+        rows = xs[mod, k]
+        acc_g[...] += jnp.dot(rows, ring_a[slot], preferred_element_type=jnp.float32)
+        acc_u[...] += jnp.dot(rows, ring_a[slot + 1], preferred_element_type=jnp.float32)
+
+    def expand(mod):
+        acc_g[...] = jnp.zeros_like(acc_g)
+        acc_u[...] = jnp.zeros_like(acc_u)
+
+        def early(k):
+            expand_step(mod, k, None)
+            start_a(mod, k + DEPTH)
+
+        loop(n_k - DEPTH, early)
+
+        def late(k):
+            expand_step(mod, k, None)
+            if mod == 0:
+                start_a(1, k - (n_k - DEPTH))
+
+        loop(n_k, late, n_k - DEPTH)
+        gate = acc_g[...]
+        hbuf[...] = (gate / (1.0 + jnp.exp(-gate)) * acc_u[...]).astype(jnp.bfloat16)
+
+    def rs_copy(mod, i, sender):
+        peer = lax.rem(m + 1 + i, n_mdl)
+        return remote(rs_send.at[mod, i], rs_recv.at[mod, sender], rss_sem.at[mod, i],
+                      rsr_sem.at[mod, sender], g, peer)
+
+    def project(mod):
+        def part(j):
+            copy_b(mod, j).wait()
+            return jnp.dot(hbuf[...], ring_b[j], preferred_element_type=jnp.float32)
+
+        def step(j):
+            rs_send[mod, j] = part(j).astype(jnp.bfloat16)
+            rs_copy(mod, j, m).start()
+            if mod == 0:
+                copy_b(1, j).start()
+
+        loop(n_mdl - 1, step)
+        own_part[mod] = part(n_mdl - 1)
+        if mod == 0:
+            copy_b(1, n_mdl - 1).start()
+
+    core = lax.rem(m, 2)
+    sibling = m + 1 - 2 * core
+    me = g * n_mdl + m
+
+    def z_peer(i):
+        return lax.rem(m + 2 * i, n_mdl)
+
+    def z_copy(mod, i, block):
+        return remote(yall.at[mod, block], yall.at[mod, block], zs_sem.at[mod, i], yr_sem.at[mod, block],
+                      g, z_peer(i + 1))
+
+    def x_copy(mod, zi, i, block):
+        return remote(yall.at[mod, block], yall.at[mod, block], xs_sem.at[mod, zi, i], yr_sem.at[mod, block],
+                      lax.rem(g + 1 + i, n_grp), m)
+
+    def c_copy(mod, gi, zi, block):
+        return remote(yall.at[mod, block], yall.at[mod, block], cs_sem.at[mod, gi, zi], yr_sem.at[mod, block],
+                      g, sibling)
+
+    def block_of(gi, zi):
+        return lax.rem(g + gi, n_grp) * n_mdl + z_peer(zi)
+
+    def finish(mod):
+        total = own_part[mod] + xraw[mod, m].astype(jnp.float32)
+        for i in range(n_mdl - 1):
+            sender = lax.rem(m + 1 + i, n_mdl)
+            rs_copy(mod, i, sender).wait_recv()
+            total += rs_recv[mod, sender].astype(jnp.float32)
+        yall[mod, me] = total.astype(jnp.bfloat16)
+        loop(n_z - 1, lambda i: z_copy(mod, i, me).start())
+        loop(n_grp - 1, lambda i: x_copy(mod, 0, i, me).start())
+        c_copy(mod, 0, 0, me).start()
+
+    def spread_grp(mod):
+        def step(zi):
+            block = block_of(0, zi)
+            z_copy(mod, zi - 1, block).wait_recv()
+            loop(n_grp - 1, lambda i: x_copy(mod, zi, i, block).start())
+            c_copy(mod, 0, zi, block).start()
+
+        loop(n_z, step, 1)
+
+    def spread_core(mod):
+        def per_z(zi):
+            def per_g(gi):
+                block = block_of(gi, zi)
+                x_copy(mod, zi, gi - 1, block).wait_recv()
+                c_copy(mod, gi, zi, block).start()
+
+            loop(n_grp, per_g, 1)
+
+        loop(n_z, per_z)
+
+    def arrive(mod):
+        def per_z(zi):
+            def per_g(gi):
+                block = lax.rem(g + gi, n_grp) * n_mdl + lax.rem(sibling + 2 * zi, n_mdl)
+                c_copy(mod, gi, zi, block).wait_recv()
+
+            loop(n_grp, per_g)
+
+        loop(n_z, per_z)
+
+    def final_norm(mod):
+        for gi in range(n_grp):
+            total = jnp.zeros((tg, 1), jnp.float32)
+            for b in range(n_mdl):
+                y = yall[mod, gi * n_mdl + b].astype(jnp.float32)
+                total += jnp.sum(y * y, axis=1, keepdims=True)
+            scale = lax.rsqrt(total / d + 1e-05)
+            for b in range(n_mdl):
+                y = yall[mod, gi * n_mdl + b].astype(jnp.float32)
+                gain = fgs[mod][:, b * cb:(b + 1) * cb].astype(jnp.float32)
+                fin[gi * tg:(gi + 1) * tg, b * cb:(b + 1) * cb] = (y * scale * gain).astype(jnp.bfloat16)
+
+    def write_out(mod):
+        rows = outs[mod].shape[0]
+        r = lax.broadcasted_iota(jnp.int32, (8, tg), 0)
+        t = lax.broadcasted_iota(jnp.int32, (8, tg), 1)
+        pick = (t == m * rows + r).astype(jnp.bfloat16)
+        for b in range(n_mdl):
+            got = jnp.dot(pick, yall[mod, g * n_mdl + b], preferred_element_type=jnp.float32)
+            outs[mod][:, b * cb:(b + 1) * cb] = got[:rows].astype(jnp.bfloat16)
+
+    tokens = fin.shape[0]
+    first_word = me * (hc * n_head)
+
+    def head_step(mod, c, carry):
+        peak, total, target = carry
+        copy_h(mod, c).wait()
+        logits = lax.dot_general(heads[mod, c], fin[...], (((1,), (1,)), ((), ())),
+                                 preferred_element_type=jnp.float32)
+        higher = jnp.maximum(peak, jnp.max(logits, axis=0, keepdims=True))
+        total = total * jnp.exp(peak - higher) + jnp.sum(jnp.exp(logits - higher), axis=0, keepdims=True)
+        word = lax.broadcasted_iota(jnp.int32, (hc, tokens), 0) + (first_word + c * hc)
+        target = target + jnp.sum(jnp.where(word == ids[...], logits, 0.0), axis=0, keepdims=True)
+        return (higher, total, target)
+
+    def head_part(mod, lo, hi, carry):
+        return lax.fori_loop(lo, hi, lambda c, carry: head_step(mod, c, carry), carry)
+
+    def nothing():
+        return (
+            jnp.full((1, tokens), -3.0e38, jnp.float32),
+            jnp.zeros((1, tokens), jnp.float32),
+            jnp.zeros((1, tokens), jnp.float32),
+        )
+
+    normed_input(0)
+    expand(0)
+    project(0)
+    normed_input(1)
+    loop(n_head, lambda c: copy_h(0, c).start(), EARLY)
+    expand(1)
+    loop(n_head, lambda c: copy_h(1, c).start())
+    finish(0)
+    project(1)
+    spread_grp(0)
+    spread_core(0)
+    finish(1)
+    arrive(0)
+    final_norm(0)
+    spread_grp(1)
+    stats = head_part(0, 0, 3, nothing())
+    spread_core(1)
+    pol = head_part(0, 3, n_head, stats)
+    write_out(0)
+    arrive(1)
+    final_norm(1)
+    ref = head_part(1, 0, n_head, nothing())
+
+    for row, value in enumerate(pol + ref):
+        st_send[0, row:row + 1, :] = value
+        st1[m, row:row + 1, :] = value
+
+    def s1_copy(i, sender):
+        return remote(st_send.at[0], st1.at[sender], s1s_sem.at[i], s1r_sem.at[sender],
+                      g, lax.rem(m + 1 + i, n_mdl))
+
+    def s2_copy(i, sender):
+        return remote(st_send.at[1], st2.at[sender], s2s_sem.at[i], s2r_sem.at[sender],
+                      lax.rem(g + 1 + i, n_grp), m)
+
+    def merge(ref, count):
+        merged = []
+        for base in (0, 3):
+            peaks = [ref[i, base:base + 1, :] for i in range(count)]
+            peak = functools.reduce(jnp.maximum, peaks)
+            total = jnp.zeros((1, tokens), jnp.float32)
+            target = jnp.zeros((1, tokens), jnp.float32)
+            for i in range(count):
+                total += ref[i, base + 1:base + 2, :] * jnp.exp(peaks[i] - peak)
+                target += ref[i, base + 2:base + 3, :]
+            merged += [peak, total, target]
+        return merged
+
+    loop(n_mdl - 1, lambda i: s1_copy(i, m).start())
+    write_out(1)
+    loop(n_mdl - 1, lambda i: s1_copy(i, lax.rem(m + 1 + i, n_mdl)).wait_recv())
+    for row, value in enumerate(merge(st1, n_mdl)):
+        st_send[1, row:row + 1, :] = value
+        st2[g, row:row + 1, :] = value
+    loop(n_grp - 1, lambda i: s2_copy(i, g).start())
+
+    for mod in (0, 1):
+        loop(n_mdl - 1, lambda i, mod=mod: hid_copy(mod, i, m).wait_send())
+        loop(n_mdl - 1, lambda i, mod=mod: rs_copy(mod, i, m).wait_send())
+        loop(n_z - 1, lambda i, mod=mod: z_copy(mod, i, me).wait_send())
+
+        def sent(zi, mod=mod):
+            loop(n_grp - 1, lambda i: x_copy(mod, zi, i, block_of(0, zi)).wait_send())
+            loop(n_grp, lambda gi: c_copy(mod, gi, zi, block_of(gi, zi)).wait_send())
+
+        loop(n_z, sent)
+    loop(n_mdl - 1, lambda i: s1_copy(i, m).wait_send())
+
+    n_roll = ratio_out.shape[0]
+    row = lax.broadcasted_iota(jnp.int32, (n_roll, n_roll), 0)
+    col = lax.broadcasted_iota(jnp.int32, (n_roll, n_roll), 1)
+    size = jnp.broadcast_to(lengths[...].astype(jnp.float32), (n_roll, n_roll))
+    ends = jnp.sum(jnp.where(col <= row, size, 0.0), axis=1, keepdims=True)
+    starts = jnp.sum(jnp.where(col < row, size, 0.0), axis=1, keepdims=True)
+    position = lax.broadcasted_iota(jnp.int32, (n_roll, tokens), 1).astype(jnp.float32)
+    held = jnp.where((position >= starts) & (position < ends), 1.0, 0.0)
+
+    loop(n_grp - 1, lambda i: s2_copy(i, lax.rem(g + 1 + i, n_grp)).wait_recv())
+    pp, ps, pt, rp, rt, rg = merge(st2, n_grp)
+    log_ratio = (pt - pp - jnp.log(ps)) - (rg - rp - jnp.log(rt))
+    ratio_out[...] = jnp.sum(held * log_ratio, axis=1, keepdims=True)
+    loop(n_grp - 1, lambda i: s2_copy(i, g).wait_send())
+
+
+def pick_head_chunks(voc):
+    for n in (5, 4, 8, 10):
+        if voc % n == 0 and (voc // n) % 16 == 0:
+            return n
+    return 0
+
+
+def fits(n_grp, n_mdl, rows, d, ff, voc, tokens):
+    if rows != 4 or n_mdl % 2 or n_mdl < 4 or n_grp < 2 or tokens > 128 or not pick_head_chunks(voc):
+        return False
+    if d % (4 * n_mdl) or (d // n_mdl) % 128 or d % 32 or (d // 8) % 128 or (d // 4) % (d // n_mdl) or ff % 16:
+        return False
+    need = 2 * (2 * DEPTH * (d // 8) * ff + ff * d + 2 * voc * d + 6 * tokens * d)
+    return need < VMEM_LIMIT
+
+
+def fused(
+    pol_hidden, ref_hidden, pol_mlp_gain, ref_mlp_gain, pol_final_gain, ref_final_gain,
+    pol_gate, pol_up, pol_down, ref_gate, ref_up, ref_down, pol_head, ref_head, token_ids, lengths,
+):
+    n_grp, n_mdl = lax.axis_size("grp"), lax.axis_size("mdl")
+    rows, d = pol_hidden.shape
+    ff, voc, tokens = pol_gate.shape[1], pol_head.shape[0], token_ids.shape[0]
+    n_k, n_head = 8, pick_head_chunks(voc)
+    tg, kc, cb, hc = rows * n_mdl, d // n_k, d // n_mdl, voc // n_head
+    n_z = n_mdl // 2
+    bf, f32 = jnp.bfloat16, jnp.float32
+    vmem = pl.BlockSpec(memory_space=pltpu.VMEM)
+    hbm = pl.BlockSpec(memory_space=pl.ANY)
+    dma = pltpu.SemaphoreType.DMA
+    out = pl.pallas_call(
+        functools.partial(fused_kernel, n_grp, n_mdl, n_k, n_head),
+        out_shape=(
+            jax.ShapeDtypeStruct((rows, d), bf),
+            jax.ShapeDtypeStruct((rows, d), bf),
+            jax.ShapeDtypeStruct((lengths.shape[0], 1), f32),
+        ),
+        in_specs=[vmem] * 6 + [hbm] * 8 + [vmem] * 2,
+        out_specs=(vmem, vmem, vmem),
+        scratch_shapes=[
+            pltpu.VMEM((2, n_mdl * 16, d // 4), bf),
+            pltpu.VMEM((2, n_k, tg, kc), bf),
+            pltpu.VMEM((2, n_mdl, tg, cb), bf),
+            pltpu.VMEM((tg, ff), f32),
+            pltpu.VMEM((tg, ff), f32),
+            pltpu.VMEM((tg, ff), bf),
+            pltpu.VMEM((2 * DEPTH, kc, ff), bf),
+            pltpu.VMEM((n_mdl, ff, cb), bf),
+            pltpu.VMEM((2, n_head, hc, d), bf),
+            pltpu.VMEM((2, n_mdl - 1, tg, cb), bf),
+            pltpu.VMEM((2, n_mdl, tg, cb), bf),
+            pltpu.VMEM((2, tg, cb), f32),
+            pltpu.VMEM((2, n_grp * n_mdl, tg, cb), bf),
+            pltpu.VMEM((tokens, d), bf),
+            pltpu.VMEM((2, 8, tokens), f32),
+            pltpu.VMEM((n_mdl, 8, tokens), f32),
+            pltpu.VMEM((n_grp, 8, tokens), f32),
+            dma((2 * DEPTH,)), dma((n_mdl,)), dma((2, n_head)),
+            dma((2, n_mdl - 1)), dma((2, n_mdl)), dma((2, n_mdl - 1)), dma((2, n_mdl)),
+            dma((2, n_z - 1)), dma((2, n_z, n_grp - 1)), dma((2, n_grp, n_z)), dma((2, n_grp * n_mdl)),
+            dma((n_mdl - 1,)), dma((n_mdl,)), dma((n_grp - 1,)), dma((n_grp,)),
+        ],
+        compiler_params=pltpu.CompilerParams(
+            collective_id=0, has_side_effects=True, vmem_limit_bytes=VMEM_LIMIT
+        ),
+    )(
+        pol_hidden.reshape(16, d // 4), ref_hidden.reshape(16, d // 4),
+        pol_mlp_gain.reshape(1, d), ref_mlp_gain.reshape(1, d),
+        pol_final_gain.reshape(1, d), ref_final_gain.reshape(1, d),
+        pol_gate, pol_up, pol_down, ref_gate, ref_up, ref_down, pol_head, ref_head,
+        token_ids.reshape(1, tokens), lengths.reshape(1, -1),
+    )
+    return (out[0], out[1], out[2].reshape(-1))
+
+
 def solution(mesh):
     placed = (
         P(("grp", "mdl"), None),
@@ -122,8 +550,16 @@
         P(),
         P(),
     )
+
+    def local(*args):
+        rows, d = args[0].shape
+        ff, voc, tokens = args[6].shape[1], args[12].shape[0], args[14].shape[0]
+        if fits(mesh.shape["grp"], mesh.shape["mdl"], rows, d, ff, voc, tokens):
+            return fused(*args)
+        return per_device(*args)
+
     return jax.shard_map(
-        per_device,
+        local,
         mesh=mesh,
         in_specs=placed,
         out_specs=(P(("grp", "mdl"), None), P(("grp", "mdl"), None), P()),

time: 352 us -> 149 us (0.42)
  waiting for transfers between devices: 158 us -> 0 us
  blocking collectives: 110 us -> 0 us
  Pallas kernels: 0 us -> 73.7 us
  local copies, waits for them, and re-layouts: 3.48 us -> 71.3 us
  matrix products: 59 us -> 0 us
  between operations: 14.6 us -> 0.64 us
  other arithmetic: 6.16 us -> 1.32 us
    all_gather x2 -> x0, waiting for transfers between devices: 99.2 us -> none  [the longest x1 52.7 us: per_device(): lax.all_gather(finals[1], ('grp', 'mdl'), axis=0, tiled=True)]
    pallas_call x0 -> x1, Pallas kernels: none -> 73.7 us  [fused(): pl.pallas_call(functools.partial(fused_kernel, n_grp, n_mdl, n_k, n_head)...]
    unnamed x21 -> x6, local copies, waits for them, and re-layouts: 3.32 us -> 63.3 us
    dot_general x6 -> x0, matrix products: 59 us -> none  [the longest x2 28 us: project(): return jnp.dot(hidden, w_down, preferred_element_type=jnp.float32)]
    unnamed x4 -> x0, waiting for transfers between devices: 59 us -> none
    psum x1 -> x0, blocking collectives: 39.8 us -> none  [per_device(): lax.psum((pol_terms[1] * jnp.exp(pol_terms[0] - peaks[0]), pol_terms[2],...]
    pmax x1 -> x0, blocking collectives: 39.5 us -> none  [per_device(): peaks = lax.pmax((pol_terms[0], ref_terms[0]), ('grp', 'mdl'))]
    all_gather x2 -> x0, blocking collectives: 30.5 us -> none  [per_device(): lax.all_gather(hidden_in, 'mdl', axis=0, tiled=True)]
  transfers between devices with their start and end apart: 3 -> 0, of which waited for: 3 -> 0; matrix products, arithmetic and copies ran while one was open for 3% -> 0% of each run, Pallas kernels for 0% -> 0%
where the time goes in v1:
time: 149 us; the launch traced here: 147 us
  Pallas kernels  73.7 us (49%)
  local copies, waits for them, and re-layouts  71.3 us (48%)
    pallas_call x1, Pallas kernels, fused(): pl.pallas_call(functools.partial(fused_kernel, n_grp, n_mdl, n_k, n_head)...  73.7 us
    unnamed x6, local copies, waits for them, and re-layouts  63.3 us

profile of v1, /device:TPU:0, one launch (start us, length us, event | category | flops | bytes accessed | tf_op | source)
XLA Modules:
  0.0 146.9 jit_solution(11658916184341582045)
XLA Ops:
  0.6 1.3 reshape.35.pol_mg
  1.9 1.3 reshape.36.ref_mg
  3.2 1.3 reshape.37.pol_fg
  4.5 1.3 reshape.38.ref_fg
  5.9 1.4 reshape.33.pol_hid
  7.3 1.4 reshape.34.ref_hid
  8.7 15.3 %copy.23.pol_gate = bf16[4096,1376]{1,0:T(8,128)(2,1)} copy(bf16[4096,1376]{0,1:T(8,128)(2,1)} %param.22) | data formatting | bytes 22544384 | tf_op args[6]
  23.9 15.1 %copy.24.pol_up = bf16[4096,1376]{1,0:T(8,128)(2,1)} copy(bf16[4096,1376]{0,1:T(8,128)(2,1)} %param.23) | data formatting | bytes 22544384 | tf_op args[7]
  39.0 15.1 %copy.25.ref_gate = bf16[4096,1376]{1,0:T(8,128)(2,1)} copy(bf16[4096,1376]{0,1:T(8,128)(2,1)} %param.25) | data formatting | bytes 22544384 | tf_op args[9]
  54.1 15.0 %copy.26.ref_up = bf16[4096,1376]{1,0:T(8,128)(2,1)} copy(bf16[4096,1376]{0,1:T(8,128)(2,1)} %param.26) | data formatting | bytes 22544384 | tf_op args[10]
  69.1 73.7 %shard_map.175 = (bf16[4,4096]{1,0:T(4,128)(2,1)}, bf16[4,4096]{1,0:T(4,128)(2,1)}, f32[16,1]{1,0:T(8,128)}) custom-call(bf16[16,1024]{1,0:T(8,128)(2,1)} %reshape.33.pol_hid, bf16[16,1024]{1,0:T(8,128)(2,1)} %reshape.34.ref_hid, bf16[1,4096]{1,0:T(2,128)(2,1)} %reshape.35.pol_mg, bf16[1,4096]{1,0:T(2,128)(2,1)} %reshape.36.ref_mg, ...), custom_call_target="tpu_custom_call" | custom-call | tf_op jit(solution)/shard_map/pallas_call | solution.py:489
  142.8 1.3 reduce
  144.2 1.4 copy.29
  145.6 1.4 copy.30

commit v2 on v1

--- a/solution.py
+++ b/solution.py
@@ -115,7 +115,7 @@
 
 def fused_kernel(
     n_grp, n_mdl, n_k, n_head,
-    pol_hid, ref_hid, pol_mg, ref_mg, pol_fg, ref_fg,
+    hidden, gains,
     pol_gate, pol_up, pol_down, ref_gate, ref_up, ref_down,
     pol_head, ref_head, ids, lengths,
     pol_out, ref_out, ratio_out,
@@ -129,21 +129,21 @@
     n_z = n_mdl // 2
     tg = xs.shape[2]
     kc = xs.shape[3]
-    d = pol_gate.shape[0]
+    d = pol_gate.shape[1]
     cb = d // n_mdl
     quarter = d // 4
     hc = pol_head.shape[0] // n_head
     gates, ups, downs = (pol_gate, ref_gate), (pol_up, ref_up), (pol_down, ref_down)
     head_refs = (pol_head, ref_head)
-    hids, mgs, fgs = (pol_hid, ref_hid), (pol_mg, ref_mg), (pol_fg, ref_fg)
+    hids = (hidden.at[0:16], hidden.at[16:32])
     outs = (pol_out, ref_out)
 
     def copy_a(mod, k):
         slot = lax.rem(k, DEPTH) * 2
-        rows = pl.ds(pl.multiple_of(k * kc, kc), kc)
+        cols = pl.ds(pl.multiple_of(k * kc, kc), kc)
         return (
-            pltpu.make_async_copy(gates[mod].at[rows, :], ring_a.at[slot], sem_a.at[slot]),
-            pltpu.make_async_copy(ups[mod].at[rows, :], ring_a.at[slot + 1], sem_a.at[slot + 1]),
+            pltpu.make_async_copy(gates[mod].at[:, cols], ring_a.at[slot], sem_a.at[slot]),
+            pltpu.make_async_copy(ups[mod].at[:, cols], ring_a.at[slot + 1], sem_a.at[slot + 1]),
         )
 
     def start_a(mod, k):
@@ -208,7 +208,7 @@
             parts.append(part)
         scale = lax.rsqrt(total / d + 1e-05)
         for q in range(4):
-            gain = mgs[mod][:, q * quarter:(q + 1) * quarter].astype(jnp.float32)
+            gain = gains[:, mod * d + q * quarter:mod * d + (q + 1) * quarter]
             normed = (parts[q] * scale * gain).astype(jnp.bfloat16)
             raw = parts[q].astype(jnp.bfloat16)
             for b in range(quarter // kc):
@@ -221,8 +221,9 @@
             c.wait()
         slot = lax.rem(k, DEPTH) * 2
         rows = xs[mod, k]
-        acc_g[...] += jnp.dot(rows, ring_a[slot], preferred_element_type=jnp.float32)
-        acc_u[...] += jnp.dot(rows, ring_a[slot + 1], preferred_element_type=jnp.float32)
+        dims = (((1,), (1,)), ((), ()))
+        acc_g[...] += lax.dot_general(rows, ring_a[slot], dims, preferred_element_type=jnp.float32)
+        acc_u[...] += lax.dot_general(rows, ring_a[slot + 1], dims, preferred_element_type=jnp.float32)
 
     def expand(mod):
         acc_g[...] = jnp.zeros_like(acc_g)
@@ -336,7 +337,7 @@
             scale = lax.rsqrt(total / d + 1e-05)
             for b in range(n_mdl):
                 y = yall[mod, gi * n_mdl + b].astype(jnp.float32)
-                gain = fgs[mod][:, b * cb:(b + 1) * cb].astype(jnp.float32)
+                gain = gains[:, (2 + mod) * d + b * cb:(2 + mod) * d + (b + 1) * cb]
                 fin[gi * tg:(gi + 1) * tg, b * cb:(b + 1) * cb] = (y * scale * gain).astype(jnp.bfloat16)
 
     def write_out(mod):
@@ -440,7 +441,7 @@
         loop(n_z, sent)
     loop(n_mdl - 1, lambda i: s1_copy(i, m).wait_send())
 
-    n_roll = ratio_out.shape[0]
+    n_roll = ratio_out.shape[1]
     row = lax.broadcasted_iota(jnp.int32, (n_roll, n_roll), 0)
     col = lax.broadcasted_iota(jnp.int32, (n_roll, n_roll), 1)
     size = jnp.broadcast_to(lengths[...].astype(jnp.float32), (n_roll, n_roll))
@@ -452,7 +453,8 @@
     loop(n_grp - 1, lambda i: s2_copy(i, lax.rem(g + 1 + i, n_grp)).wait_recv())
     pp, ps, pt, rp, rt, rg = merge(st2, n_grp)
     log_ratio = (pt - pp - jnp.log(ps)) - (rg - rp - jnp.log(rt))
-    ratio_out[...] = jnp.sum(held * log_ratio, axis=1, keepdims=True)
+    ratio = jnp.sum(held * log_ratio, axis=1, keepdims=True)
+    ratio_out[...] = jnp.sum(jnp.where(row == col, ratio, 0.0), axis=0, keepdims=True)
     loop(n_grp - 1, lambda i: s2_copy(i, g).wait_send())
 
 
@@ -491,9 +493,9 @@
         out_shape=(
             jax.ShapeDtypeStruct((rows, d), bf),
             jax.ShapeDtypeStruct((rows, d), bf),
-            jax.ShapeDtypeStruct((lengths.shape[0], 1), f32),
+            jax.ShapeDtypeStruct((1, lengths.shape[0]), f32),
         ),
-        in_specs=[vmem] * 6 + [hbm] * 8 + [vmem] * 2,
+        in_specs=[vmem] * 2 + [hbm] * 8 + [vmem] * 2,
         out_specs=(vmem, vmem, vmem),
         scratch_shapes=[
             pltpu.VMEM((2, n_mdl * 16, d // 4), bf),
@@ -502,7 +504,7 @@
             pltpu.VMEM((tg, ff), f32),
             pltpu.VMEM((tg, ff), f32),
             pltpu.VMEM((tg, ff), bf),
-            pltpu.VMEM((2 * DEPTH, kc, ff), bf),
+            pltpu.VMEM((2 * DEPTH, ff, kc), bf),
             pltpu.VMEM((n_mdl, ff, cb), bf),
             pltpu.VMEM((2, n_head, hc, d), bf),
             pltpu.VMEM((2, n_mdl - 1, tg, cb), bf),
@@ -522,10 +524,9 @@
             collective_id=0, has_side_effects=True, vmem_limit_bytes=VMEM_LIMIT
         ),
     )(
-        pol_hidden.reshape(16, d // 4), ref_hidden.reshape(16, d // 4),
-        pol_mlp_gain.reshape(1, d), ref_mlp_gain.reshape(1, d),
-        pol_final_gain.reshape(1, d), ref_final_gain.reshape(1, d),
-        pol_gate, pol_up, pol_down, ref_gate, ref_up, ref_down, pol_head, ref_head,
+        jnp.concatenate([pol_hidden, ref_hidden]).reshape(32, d // 4),
+        jnp.concatenate([pol_mlp_gain, ref_mlp_gain, pol_final_gain, ref_final_gain]).astype(f32).reshape(1, 4 * d),
+        pol_gate.T, pol_up.T, pol_down, ref_gate.T, ref_up.T, ref_down, pol_head, ref_head,
         token_ids.reshape(1, tokens), lengths.reshape(1, -1),
     )
     return (out[0], out[1], out[2].reshape(-1))

time: 149 us -> 85 us (0.57)
  local copies, waits for them, and re-layouts: 71.3 us -> 7.4 us
    unnamed x6 -> x3, local copies, waits for them, and re-layouts: 63.3 us -> 3.9 us
    reshape x6 -> x1, local copies, waits for them, and re-layouts: 8.02 us -> 0.67 us  [fused(): jnp.concatenate([pol_hidden, ref_hidden]).reshape(32, d // 4)]
    concatenate x0 -> x4, local copies, waits for them, and re-layouts: none -> 2.84 us  [fused(): jnp.concatenate([pol_mlp_gain, ref_mlp_gain, pol_final_gain, ref_final_ga...]
where the time goes in v2:
time: 85 us; the launch traced here: 84.4 us
  Pallas kernels  74.9 us (88%)
  local copies, waits for them, and re-layouts  7.4 us (9%)
  other arithmetic  1.5 us (2%)
    pallas_call x1, Pallas kernels, fused(): pl.pallas_call(functools.partial(fused_kernel, n_grp, n_mdl, n_k, n_head)...  74.9 us
    unnamed x3, local copies, waits for them, and re-layouts  3.9 us
    concatenate x4, local copies, waits for them, and re-layouts, fused(): jnp.concatenate([pol_mlp_gain, ref_mlp_gain, pol_final_gain, ref_final_ga...  2.84 us

profile of v2, /device:TPU:0, one launch (start us, length us, event | category | flops | bytes accessed | tf_op | source)
XLA Modules:
  0.0 84.4 jit_solution(7648397777375377680)
XLA Ops:
  0.6 0.7 concatenate.22
  1.3 0.7 concatenate.23
  2.1 0.7 concatenate.24
  2.8 0.7 concatenate.25
  3.5 0.7 maximum_convert_fusion.gains
  4.2 0.8 pad_maximum_fusion
  5.0 0.7 reshape.74.hidden
  5.7 74.9 %shard_map.175 = (bf16[4,4096]{1,0:T(4,128)(2,1)}, bf16[4,4096]{1,0:T(4,128)(2,1)}, f32[1,16]{1,0:T(1,128)}) custom-call(bf16[32,1024]{1,0:T(8,128)(2,1)} %reshape.74.hidden, f32[1,16384]{1,0:T(1,128)} %maximum_convert_fusion.gains, bf16[1376,4096]{1,0:T(8,128)(2,1)} %bitcast.7, bf16[1376,4096]{1,0:T(8,128)(2,1)} %bitcast.8, bf16[1376,4096]{1,0:T(8,128)(2,1)} %pol_down.1, ...), custom_call_target="tpu_custom_call" | custom-call | tf_op jit(solution)/shard_map/pallas_call | solution.py:491
  80.5 1.4 %copy.22 = bf16[4,4096]{1,0:T(4,128)(2,1)} copy(bf16[4,4096]{1,0:T(4,128)(2,1)} %get-tuple-element.12) | data formatting | bytes 65536
  81.9 1.4 %copy.23 = bf16[4,4096]{1,0:T(4,128)(2,1)} copy(bf16[4,4096]{1,0:T(4,128)(2,1)} %get-tuple-element.13) | data formatting | bytes 65536
  83.3 1.1 %copy.24 = f32[16]{0:T(128)} copy(f32[16]{0:T(128)} %bitcast.13) | data formatting | bytes 128
